TPU v7x, 32 devices: a whole 2x2x4 slice. The times are simulated.
32 devices in a mesh: row: 4 (over y, core), col: 8 (over z, x).
Axes of the slice: x: 2, y: 2, z: 4, core: 2. Of those that a mesh axis runs over, the one named last changes fastest.
Arguments:
- leaf_rhs: bfloat16 [4, 64, 2048], P('row', 'col'), may hold values from -6 to 6
- leaf_inverse: bfloat16 [4, 2048, 2048], P('row'), may hold values from -0.125 to 0.125
- interpolation: bfloat16 [4, 128, 2048], P('row'), may hold values from -0.5 to 0.5
- ranks: int32 [4], P('row'), may hold values from 32 to 128, as said below
- skeleton_rows: int32 [4, 128], P('row'), may hold values from 0 to 2047, as said below
- root_rows: int32 [4, 128], replicated, may hold values from 0 to 16383, as said below
- root_rhs: float32 [64, 16384], P('col', 'row'), may hold values from -6 to 6
- root_factor: bfloat16 [16384, 4, 4096], P('row', None, 'col')
Outputs:
- leaf_solution: float32 [4, 64, 2048], P('row', 'col')
- root_solution: float32 [64, 16384], P('col', 'row')
Inputs may be any that keep to these rules, and one draw needn't show every extreme that they name: `ranks`: some leaf has rank 128. `skeleton_rows`: distinct within each leaf. `root_rows`: all distinct over all leaves and slots.
All inputs are finite; a program needn't handle non-finite values.
Results may differ from a plain program's by a relative error of at most 0.014.
Values may be sent and summed in bfloat16 or wider, within the bound.
A program may use at most 128 MiB of HBM per device.

v0:
```python
import jax
import jax.numpy as jnp
from jax import lax
from jax.sharding import PartitionSpec as P


def from_root(value, axis, source):
    kept = jnp.where(lax.axis_index(axis) == source, value, 0).astype(value.dtype)
    return lax.psum(kept, axis)


def product_rows(left_rows, factor_rows):
    return lax.dot_general(
        left_rows, factor_rows, (((1,), (1,)), ((), ())), preferred_element_type=jnp.float32
    )


def folder(factor_block, piece):
    return product_rows(piece, factor_block)


def on_device(
    leaf_rhs, leaf_inverse, interpolation, ranks, skeleton_rows, root_rows, root_rhs, root_factor
):
    row_at = lax.axis_index("row")
    row_count = lax.axis_size("row")
    leaf_here = leaf_rhs.shape[0]
    rhs_here = leaf_rhs.shape[1]
    slot_count = skeleton_rows.shape[1]
    section = root_rhs.shape[1]
    solved = jnp.einsum("lrk,ljk->lrj", leaf_rhs, leaf_inverse, preferred_element_type=jnp.float32)
    live_slots = jnp.arange(slot_count, dtype=jnp.int32)[None, :] < ranks[:, None]
    index_table = jnp.broadcast_to(skeleton_rows[:, None, :], (leaf_here, rhs_here, slot_count))
    skeleton = jnp.where(
        live_slots[:, None, :], jnp.take_along_axis(solved, index_table, axis=2), 0.0
    )
    gathered_skel = lax.all_gather(skeleton, "row", axis=0, tiled=True)
    flat_values = jnp.transpose(gathered_skel, (1, 0, 2)).reshape(rhs_here, -1)
    local_rows = root_rows.reshape(-1) - row_at * section
    inside = (local_rows >= 0) & (local_rows < section)
    target = jnp.where(inside, local_rows, section)
    assembled = root_rhs.at[:, target].add(flat_values, mode="drop")
    relaid = lax.all_to_all(root_factor, "col", split_axis=0, concat_axis=2, tiled=True)
    running = lax.all_to_all(assembled, "col", split_axis=1, concat_axis=0, tiled=True)
    for block_index in range(row_count):
        factor_block = relaid[:, block_index, :]
        arrived = from_root(running.astype(jnp.bfloat16), "row", block_index)
        update = folder(factor_block, lax.all_gather(arrived, "col", axis=1, tiled=True))
        running = jnp.where(row_at > block_index, running - update, running)
    result = jnp.zeros_like(running)
    for block_index in reversed(range(row_count)):
        factor_block = relaid[:, block_index, :]
        diagonal_out = folder(
            factor_block, lax.all_gather(running.astype(jnp.bfloat16), "col", axis=1, tiled=True)
        )
        result = jnp.where(row_at == block_index, diagonal_out, result)
        arrived = from_root(diagonal_out.astype(jnp.bfloat16), "row", block_index)
        update = folder(factor_block, lax.all_gather(arrived, "col", axis=1, tiled=True))
        running = jnp.where(row_at < block_index, running - update, running)
    root_solution = lax.all_to_all(result, "col", split_axis=0, concat_axis=1, tiled=True)
    gathered_rows = lax.all_gather(root_solution.astype(jnp.bfloat16), "row", axis=1, tiled=True)
    own_targets = lax.dynamic_slice_in_dim(root_rows, row_at * leaf_here, leaf_here, 0)
    taken = jnp.take(gathered_rows, own_targets.reshape(-1), axis=1).reshape(
        rhs_here, leaf_here, slot_count
    )
    skeleton_low = jnp.transpose(taken, (1, 0, 2))
    skeleton_solution = jnp.where(
        live_slots[:, None, :], skeleton_low, jnp.zeros_like(skeleton_low)
    )
    correction = jnp.einsum(
        "lrk,lkj->lrj", skeleton_solution, interpolation, preferred_element_type=jnp.float32
    )
    leaf_solution = solved - correction
    return (leaf_solution, root_solution)


def solution(mesh):
    in_specs = (
        P("row", "col", None),
        P("row", None, None),
        P("row", None, None),
        P("row"),
        P("row", None),
        P(),
        P("col", "row"),
        P("row", None, "col"),
    )
    out_specs = (P("row", "col", None), P("col", "row"))
    return jax.shard_map(
        on_device, mesh=mesh, in_specs=in_specs, out_specs=out_specs, check_vma=False
    )
```

profile of v0, /device:TPU:0, one launch (start us, length us, event | category | flops | bytes accessed | tf_op | source)
XLA Modules:
  0.0 1067.3 jit_solution(7169760882724766798)
XLA Ops:
  7.9 0.7 broadcast_add_fusion
  8.6 0.7 iota_compare_fusion
  9.2 0.7 broadcast_subtract_fusion
  9.9 5.7 fusion
  15.6 6.8 gather_fusion.1
  22.4 6.2 all_gather.39
  29.4 4.1 scatter_fusion
  34.0 13.5 %all_to_all.56 = f32[8,8,512]{2,0,1:T(8,128)S(1)} all-to-all(f32[8,8,512]{2,0,1:T(8,128)S(1)} %copy.35), channel_id=1, replica_groups=mesh['row'=4,'col'=8] {'col'}, dimensions={1} | all-to-all | bytes 262144 | tf_op jit(solution)/shard_map/all_to_all | solution.py:44
  47.5 5.7 all-to-all-start.1
  53.3 0.6 fusion.32
  54.0 35.3 %all-reduce.8.cloned.1.call-done = bf16[64,512]{1,0:T(8,128)(2,1)} async-done(((bf16[64,512]{1,0:T(8,128)(2,1)}), bf16[64,512]{1,0:T(8,128)(2,1)}) %all-reduce.8.cloned.1.call-update) | async-done | bytes 65552 | tf_op jit(solution)/shard_map/psum | solution.py:9
  89.4 347.0 %all_gather.40 = bf16[64,4096]{1,0:T(8,128)(2,1)S(1)} all-gather(bf16[64,512]{1,0:T(8,128)(2,1)} %all-reduce.8.cloned.1.call-done), channel_id=1, replica_groups=mesh['row'=4,'col'=8] {'col'}, dimensions={1}, use_global_device_ids=true | all-gather | bytes 589824 | tf_op jit(solution)/shard_map/all_gather | solution.py:48
  436.3 16.3 %copy.36 = bf16[4096,4,512]{2,0,1:T(8,128)(2,1)} copy(bf16[4096,4,512]{2,1,0:T(4,128)(2,1)} %all-to-all-done.1) | data formatting | bytes 33554432 | tf_op jit(solution)/shard_map/all_to_all | solution.py:43
  452.6 21.8 %copy.37 = bf16[512,4,8,512]{0,3,2,1:T(8,128)(2,1)} copy(bf16[512,4,8,512]{3,0,2,1:T(8,128)(2,1)} %bitcast.145) | data formatting | bytes 33554432 | tf_op jit(solution)/shard_map/all_to_all | solution.py:43
  474.4 3.7 convert_select_fusion.5
  478.2 30.5 %all-reduce.10.cloned.1.call-done = bf16[64,512]{1,0:T(8,128)(2,1)} async-done(((bf16[64,512]{1,0:T(8,128)(2,1)}), bf16[64,512]{1,0:T(8,128)(2,1)}) %all-reduce.10.cloned.1.call-update) | async-done | bytes 65552 | tf_op jit(solution)/shard_map/psum | solution.py:9
  508.7 31.6 %all_gather.41 = bf16[64,4096]{1,0:T(8,128)(2,1)S(1)} all-gather(bf16[64,512]{1,0:T(8,128)(2,1)} %all-reduce.10.cloned.1.call-done), channel_id=1, replica_groups=mesh['row'=4,'col'=8] {'col'}, dimensions={1}, use_global_device_ids=true | all-gather | bytes 589824 | tf_op jit(solution)/shard_map/all_gather | solution.py:48
  540.3 3.7 convert_select_fusion.4
  544.0 31.0 %all-reduce.12.cloned.1.call-done = bf16[64,512]{1,0:T(8,128)(2,1)} async-done(((bf16[64,512]{1,0:T(8,128)(2,1)}), bf16[64,512]{1,0:T(8,128)(2,1)}) %all-reduce.12.cloned.1.call-update) | async-done | bytes 65552 | tf_op jit(solution)/shard_map/psum | solution.py:9
  575.0 31.6 %all_gather.42 = bf16[64,4096]{1,0:T(8,128)(2,1)S(1)} all-gather(bf16[64,512]{1,0:T(8,128)(2,1)} %all-reduce.12.cloned.1.call-done), channel_id=1, replica_groups=mesh['row'=4,'col'=8] {'col'}, dimensions={1}, use_global_device_ids=true | all-gather | bytes 589824 | tf_op jit(solution)/shard_map/all_gather | solution.py:48
  606.6 3.7 convert_select_fusion.3
  610.3 31.1 %all-reduce.14.cloned.1.call-done = bf16[64,512]{1,0:T(8,128)(2,1)} async-done(((bf16[64,512]{1,0:T(8,128)(2,1)}), bf16[64,512]{1,0:T(8,128)(2,1)}) %all-reduce.14.cloned.1.call-update) | async-done | bytes 65552 | tf_op jit(solution)/shard_map/psum | solution.py:9
  641.4 31.6 %all_gather.43 = bf16[64,4096]{1,0:T(8,128)(2,1)S(1)} all-gather(bf16[64,512]{1,0:T(8,128)(2,1)} %all-reduce.14.cloned.1.call-done), channel_id=1, replica_groups=mesh['row'=4,'col'=8] {'col'}, dimensions={1}, use_global_device_ids=true | all-gather | bytes 589824 | tf_op jit(solution)/shard_map/all_gather | solution.py:48
  673.0 3.0 fusion.45
  676.0 31.3 %all_gather.44 = bf16[64,4096]{1,0:T(8,128)(2,1)S(1)} all-gather(bf16[64,512]{1,0:T(8,128)(2,1)S(1)} %get-tuple-element.16), channel_id=1, replica_groups=mesh['row'=4,'col'=8] {'col'}, dimensions={1}, use_global_device_ids=true | all-gather | bytes 589824 | tf_op jit(solution)/shard_map/all_gather | solution.py:54
  707.3 3.7 convert_select_fusion.2
  711.0 31.2 %all-reduce.16.cloned.1.call-done = bf16[64,512]{1,0:T(8,128)(2,1)} async-done(((bf16[64,512]{1,0:T(8,128)(2,1)}), bf16[64,512]{1,0:T(8,128)(2,1)}) %all-reduce.16.cloned.1.call-update) | async-done | bytes 65552 | tf_op jit(solution)/shard_map/psum | solution.py:9
  742.2 31.7 %all_gather.45 = bf16[64,4096]{1,0:T(8,128)(2,1)S(1)} all-gather(bf16[64,512]{1,0:T(8,128)(2,1)} %all-reduce.16.cloned.1.call-done), channel_id=1, replica_groups=mesh['row'=4,'col'=8] {'col'}, dimensions={1}, use_global_device_ids=true | all-gather | bytes 589824 | tf_op jit(solution)/shard_map/all_gather | solution.py:58
  773.9 3.0 fusion.46
  777.0 31.3 %all_gather.46 = bf16[64,4096]{1,0:T(8,128)(2,1)S(1)} all-gather(bf16[64,512]{1,0:T(8,128)(2,1)S(1)} %get-tuple-element.20), channel_id=1, replica_groups=mesh['row'=4,'col'=8] {'col'}, dimensions={1}, use_global_device_ids=true | all-gather | bytes 589824 | tf_op jit(solution)/shard_map/all_gather | solution.py:54
  808.3 3.7 convert_select_fusion.1
  812.0 31.1 %all-reduce.18.cloned.1.call-done = bf16[64,512]{1,0:T(8,128)(2,1)} async-done(((bf16[64,512]{1,0:T(8,128)(2,1)}), bf16[64,512]{1,0:T(8,128)(2,1)}) %all-reduce.18.cloned.1.call-update) | async-done | bytes 65552 | tf_op jit(solution)/shard_map/psum | solution.py:9
  843.2 31.6 %all_gather.47 = bf16[64,4096]{1,0:T(8,128)(2,1)S(1)} all-gather(bf16[64,512]{1,0:T(8,128)(2,1)} %all-reduce.18.cloned.1.call-done), channel_id=1, replica_groups=mesh['row'=4,'col'=8] {'col'}, dimensions={1}, use_global_device_ids=true | all-gather | bytes 589824 | tf_op jit(solution)/shard_map/all_gather | solution.py:58
  874.7 3.0 fusion.47
  877.8 31.3 %all_gather.48 = bf16[64,4096]{1,0:T(8,128)(2,1)S(1)} all-gather(bf16[64,512]{1,0:T(8,128)(2,1)S(1)} %get-tuple-element.24), channel_id=1, replica_groups=mesh['row'=4,'col'=8] {'col'}, dimensions={1}, use_global_device_ids=true | all-gather | bytes 589824 | tf_op jit(solution)/shard_map/all_gather | solution.py:54
  909.0 3.7 convert_select_fusion
  912.8 31.2 %all-reduce.20.cloned.1.call-done = bf16[64,512]{1,0:T(8,128)(2,1)} async-done(((bf16[64,512]{1,0:T(8,128)(2,1)}), bf16[64,512]{1,0:T(8,128)(2,1)}) %all-reduce.20.cloned.1.call-update) | async-done | bytes 65552 | tf_op jit(solution)/shard_map/psum | solution.py:9
  943.9 31.6 %all_gather.49 = bf16[64,4096]{1,0:T(8,128)(2,1)S(1)} all-gather(bf16[64,512]{1,0:T(8,128)(2,1)} %all-reduce.20.cloned.1.call-done), channel_id=1, replica_groups=mesh['row'=4,'col'=8] {'col'}, dimensions={1}, use_global_device_ids=true | all-gather | bytes 589824 | tf_op jit(solution)/shard_map/all_gather | solution.py:58
  975.5 3.0 fusion.28
  978.5 31.3 %all_gather.50 = bf16[64,4096]{1,0:T(8,128)(2,1)S(1)} all-gather(bf16[64,512]{1,0:T(8,128)(2,1)S(1)} %fusion.28), channel_id=1, replica_groups=mesh['row'=4,'col'=8] {'col'}, dimensions={1}, use_global_device_ids=true | all-gather | bytes 589824 | tf_op jit(solution)/shard_map/all_gather | solution.py:54
  1009.8 3.7 fusion.30
  1013.5 5.4 all-to-all-start.2
  1018.9 7.3 all-to-all-done.2
  1026.8 1.1 bitcast_convert_fusion.1
  1027.9 1.2 copy.43
  1029.1 27.0 %all_gather.51 = bf16[8,16384]{0,1:T(8,128)(2,1)} all-gather(bf16[8,4096]{0,1:T(8,128)(2,1)} %bitcast_convert_fusion.1), channel_id=1, replica_groups=mesh['row'=4,'col'=8] {'row'}, dimensions={1}, use_global_device_ids=true | all-gather | bytes 327680 | tf_op jit(solution)/shard_map/all_gather | solution.py:61
  1056.1 3.4 gather_fusion
  1059.5 0.9 fusion.13
  (33 shorter events, 2.4 us)
Async XLA Ops:
  7.2 1052.3 %copy-start = (bf16[1,128,2048]{2,1,0:T(8,128)(2,1)S(1)}, bf16[1,128,2048]{2,1,0:T(8,128)(2,1)}, u32[]{:S(2)}) copy-start(bf16[1,128,2048]{2,1,0:T(8,128)(2,1)} %param.10) | copy-start | bytes 1572868
  7.2 8.4 copy-start.2
  7.2 21.6 %copy-start.1 = (f32[8,4096]{1,0:T(8,128)S(1)}, f32[8,4096]{1,0:T(8,128)}, u32[]{:S(2)}) copy-start(f32[8,4096]{1,0:T(8,128)} %param.14) | copy-start | bytes 393220
  47.5 388.9 %all-to-all-start.1 = ((bf16[4096,4,512]{2,1,0:T(4,128)(2,1)}), bf16[4096,4,512]{2,1,0:T(4,128)(2,1)}, u32[]{:S(2)}, u32[]{:S(2)}) async-start(bf16[4096,4,512]{2,1,0:T(4,128)(2,1)} %param.15), calls=%async_computation.1 | async-start | bytes 33554432 | tf_op jit(solution)/shard_map/all_to_all | solution.py:43
  53.2 36.1 %all-reduce.8.cloned.1.call-start = ((), (), s32[]{:S(2)}) async-start(), calls=%async_computation.3 | async-start | bytes 131072 | tf_op jit(solution)/shard_map/psum | solution.py:9
  54.0 454.7 %all-reduce.10.cloned.1.call-start = ((), (), s32[]{:S(2)}) async-start(), calls=%async_computation.4 | async-start | bytes 131072 | tf_op jit(solution)/shard_map/psum | solution.py:9
  478.1 96.9 %all-reduce.12.cloned.1.call-start = ((), (), s32[]{:S(2)}) async-start(), calls=%async_computation.5 | async-start | bytes 131072 | tf_op jit(solution)/shard_map/psum | solution.py:9
  544.0 97.4 %all-reduce.14.cloned.1.call-start = ((), (), s32[]{:S(2)}) async-start(), calls=%async_computation.6 | async-start | bytes 131072 | tf_op jit(solution)/shard_map/psum | solution.py:9
  610.3 131.9 %all-reduce.16.cloned.1.call-start = ((), (), s32[]{:S(2)}) async-start(), calls=%async_computation.7 | async-start | bytes 131072 | tf_op jit(solution)/shard_map/psum | solution.py:9
  711.0 132.2 %all-reduce.18.cloned.1.call-start = ((), (), s32[]{:S(2)}) async-start(), calls=%async_computation.8 | async-start | bytes 131072 | tf_op jit(solution)/shard_map/psum | solution.py:9
  812.0 132.0 %all-reduce.20.cloned.1.call-start = ((), (), s32[]{:S(2)}) async-start(), calls=%async_computation.9 | async-start | bytes 131072 | tf_op jit(solution)/shard_map/psum | solution.py:9
  909.0 109.8 %copy-start.3 = (s32[4,128]{1,0:T(4,128)S(1)}, s32[4,128]{1,0:T(4,128)}, u32[]{:S(2)}) copy-start(s32[4,128]{1,0:T(4,128)} %param.13) | copy-start | bytes 6148
  1013.5 12.7 %all-to-all-start.2 = ((f32[8,8,512]{2,1,0:T(8,128)}), f32[8,8,512]{2,1,0:T(8,128)S(1)}, u32[]{:S(2)}, u32[]{:S(2)}) async-start(f32[8,8,512]{2,1,0:T(8,128)} %fusion.30), calls=%async_computation.2 | async-start | bytes 262144 | tf_op jit(solution)/shard_map/all_to_all | solution.py:60
Sparse Core Ops, SparseCore 0:
  56.9 32.3 all-reduce.7
  478.2 30.4 all-reduce.9
  544.1 30.8 all-reduce.11
  610.4 30.9 all-reduce.13
  711.1 31.0 all-reduce.15
  812.1 31.0 all-reduce.17
  912.9 31.0 all-reduce.19
where the time goes:
time: 1070 us
  blocking collectives  708 us (66%)
  waiting for transfers between devices  229 us (21%)
  local copies, waits for them, and re-layouts  51.4 us (5%)
  matrix products  44.4 us (4%)
  between operations  15 us (1%)
  starting transfers between devices  11.4 us (1%)
    all_gather x7, blocking collectives, on_device(): lax.all_gather(arrived, 'col', axis=1, tiled=True)  537 us
    psum x7, waiting for transfers between devices, from_root(): return lax.psum(kept, axis)  221 us
    all_gather x4, blocking collectives, on_device(): lax.all_gather(running.astype(jnp.bfloat16), 'col', axis=1, tiled=True)  125 us
    all_to_all x2, local copies, waits for them, and re-layouts, on_device(): lax.all_to_all(root_factor, 'col', split_axis=0, concat_axis=2, tiled=True)  38.1 us
    dot_general x11, matrix products, product_rows(): lax.dot_general(left_rows, factor_rows, (((1,), (1,)), ((), ())), preferr...  37.8 us
    all_gather x1, blocking collectives, on_device(): lax.all_gather(root_solution.astype(jnp.bfloat16), 'row', axis=1, tiled=T...  27 us
  transfers between devices with their start and end apart: 9, of which 8 were waited for; matrix products, arithmetic and copies ran while one was open for 0% of the time, Pallas kernels for 0%

commit v1 on v0

v1 whole, which is shorter than its diff:
```python
import functools

import jax
import jax.numpy as jnp
from jax import lax
from jax.experimental import pallas as pl
from jax.experimental.pallas import tpu as pltpu
from jax.sharding import PartitionSpec as P

BF16 = jnp.bfloat16
F32 = jnp.float32


def dot_nt(left, right):
    return lax.dot_general(left, right, (((1,), (1,)), ((), ())), preferred_element_type=F32)


def dot_nn(left, right):
    return lax.dot_general(left, right, (((1,), (0,)), ((), ())), preferred_element_type=F32)


def hi_lo(value):
    high = value.astype(BF16)
    low = (value - high.astype(F32)).astype(BF16)
    return jnp.concatenate([high, low], axis=0)


def kernel(
    rows, cols,
    ranks, leaf_rhs, leaf_inverse, interpolation, skeleton_rows, root_rows, root_rhs, factor,
    leaf_out, root_out,
    inverse_v, factor_v, hot, solved, skel_box, assem, assem_box, vec_send, vec_box,
    acc, stage, box, kept, full, sol_box, take, take_box,
    inverse_sem, factor_sem, skel_send_sem, skel_sem, assem_send_sem, assem_sem,
    vec_send_sem, vec_sem, rs_send_sem, rs_sem, sol_send_sem, sol_sem, take_send_sem, take_sem,
):
    row = lax.axis_index("row")
    col = lax.axis_index("col")
    rhs_here, section = root_rhs.shape
    width = section // cols
    slots = skeleton_rows.shape[1]
    leaf = leaf_rhs.shape[1]

    load_inverse = pltpu.make_async_copy(leaf_inverse, inverse_v, inverse_sem)
    load_inverse.start()
    load_factor = pltpu.make_async_copy(factor, factor_v, factor_sem)
    load_factor.start()

    barrier = pltpu.get_barrier_semaphore()
    for step in range(1, rows):
        pl.semaphore_signal(barrier, inc=1, device_id={"row": lax.rem(row + step, rows)})
    for step in range(1, cols):
        pl.semaphore_signal(barrier, inc=1, device_id={"col": lax.rem(col + step, cols)})

    def build_hot(part, carry):
        start = part * width
        at = lax.broadcasted_iota(jnp.int32, (width, slots), 0) + (start + row * section)
        for leaf_index in range(rows):
            wanted = root_rows[leaf_index:leaf_index + 1, :]
            hot[pl.ds(pl.multiple_of(start, width), width),
                leaf_index * slots:(leaf_index + 1) * slots] = jnp.where(
                    at == wanted, 1.0, 0.0).astype(BF16)
        return carry

    lax.fori_loop(0, cols, build_hot, 0)

    live = lax.broadcasted_iota(jnp.int32, (rhs_here, slots), 1) < ranks[0]

    load_inverse.wait()
    leaf_step = 256
    here = leaf_rhs[...]
    skeleton = jnp.zeros((2 * rhs_here, slots), F32)
    for start in range(0, leaf, leaf_step):
        part = dot_nt(here, inverse_v[start:start + leaf_step, :])
        solved[:, start:start + leaf_step] = part
        at = lax.broadcasted_iota(jnp.int32, (leaf_step, slots), 0) + start
        pick = jnp.where(at == skeleton_rows[...], 1.0, 0.0).astype(BF16)
        skeleton = skeleton + dot_nn(hi_lo(part), pick)
    skeleton = jnp.where(live, skeleton[:rhs_here] + skeleton[rhs_here:], 0.0)
    skel_box[row] = skeleton

    pl.semaphore_wait(barrier, rows + cols - 2)

    def skel_copy(target, source):
        return pltpu.make_async_remote_copy(
            skel_box.at[row], skel_box.at[source], skel_send_sem.at[target],
            skel_sem.at[source], device_id={"row": target})

    for step in range(1, rows):
        target = lax.rem(row + step, rows)
        pltpu.make_async_remote_copy(
            skel_box.at[row], skel_box.at[row], skel_send_sem.at[target],
            skel_sem.at[row], device_id={"row": target}).start()
    for step in range(1, rows):
        source = lax.rem(row + step, rows)
        skel_copy(source, source).wait_recv()

    split = [hi_lo(skel_box[leaf_index]) for leaf_index in range(rows)]
    flat = jnp.concatenate(split, axis=1)

    def assem_copy(target, slot):
        return pltpu.make_async_remote_copy(
            assem.at[target], assem_box.at[slot], assem_send_sem.at[target],
            assem_sem.at[slot], device_id={"col": target})

    def build_assem(step, carry):
        target = lax.rem(col + step, cols)
        start = pl.multiple_of(target * width, width)
        added = dot_nt(flat, hot[pl.ds(start, width), :])
        assem[target] = root_rhs[:, pl.ds(start, width)] + (added[:rhs_here] + added[rhs_here:])

        @pl.when(step < cols)
        def _():
            assem_copy(target, col).start()

        return carry

    lax.fori_loop(1, cols + 1, build_assem, 0)
    assem_box[col] = assem[col]

    def take_assem(step, carry):
        source = lax.rem(col + step, cols)
        assem_copy(source, source).wait_recv()
        return carry

    lax.fori_loop(1, cols, take_assem, 0)
    for source in range(cols):
        kept[source * rhs_here:(source + 1) * rhs_here, :] = assem_box[source]

    load_factor.wait()

    def vec_copy(kind, target, slot):
        return pltpu.make_async_remote_copy(
            vec_send.at[kind], vec_box.at[kind, slot], vec_send_sem.at[kind, target],
            vec_sem.at[kind, slot], device_id={"row": target})

    def clear():
        def body(part, carry):
            acc[part] = jnp.zeros(acc.shape[1:], F32)
            return carry
        lax.fori_loop(0, cols, body, 0)

    def block(source, part):
        return factor_v[source, pl.ds(pl.multiple_of(part * width, width), width), :]

    def gather_in(kind, source):
        vec_copy(kind, source, source).wait_recv()

        def body(part, carry):
            acc[part] += dot_nt(vec_box[kind, source], block(source, part))
            return carry

        lax.fori_loop(0, cols, body, 0)

    def rs_copy(phase, target, slot):
        return pltpu.make_async_remote_copy(
            stage.at[phase, target], box.at[phase, slot], rs_send_sem.at[phase, target],
            rs_sem.at[phase, slot], device_id={"col": target})

    def reduce_scatter(phase, vector, source, with_acc):
        def send(step, carry):
            target = lax.rem(col + step, cols)
            part = dot_nt(vector(), block(source, target))
            if with_acc:
                part = part + acc[target]
            stage[phase, target] = part.astype(BF16)
            rs_copy(phase, target, col).start()
            return carry

        lax.fori_loop(1, cols, send, 0)
        total = dot_nt(vector(), block(source, col))
        if with_acc:
            total = total + acc[col]
        full[...] = total

        def receive(step, carry):
            origin = lax.rem(col + cols - step, cols)
            rs_copy(phase, origin, origin).wait_recv()
            full[...] += box[phase, origin].astype(F32)
            return carry

        lax.fori_loop(1, cols, receive, 0)

    @pl.when(row > 0)
    def _():
        clear()

        def body(source, carry):
            gather_in(0, source)
            return carry

        lax.fori_loop(0, row - 1, body, 0)
        vec_copy(0, row - 1, row - 1).wait_recv()
        reduce_scatter(0, lambda: vec_box[0, row - 1], row - 1, True)
        kept[...] = kept[...] - full[...]

    vec_send[0] = kept[...].astype(BF16)
    for step in range(1, rows):
        @pl.when(row + step < rows)
        def _():
            vec_copy(0, row + step, row).start()

    @pl.when(row < rows - 1)
    def _():
        clear()

        def body(step, carry):
            gather_in(1, rows - 1 - step)
            return carry

        lax.fori_loop(0, rows - 2 - row, body, 0)
        vec_copy(1, row + 1, row + 1).wait_recv()
        reduce_scatter(1, lambda: vec_box[1, row + 1], row + 1, True)
        kept[...] = kept[...] - full[...]

    vec_send[2] = kept[...].astype(BF16)
    reduce_scatter(2, lambda: vec_send[2], row, False)
    vec_send[1] = full[...].astype(BF16)
    for step in range(1, rows):
        @pl.when(row - step >= 0)
        def _():
            vec_copy(1, row - step, row).start()

    def sol_copy(target, slot):
        return pltpu.make_async_remote_copy(
            full.at[pl.ds(pl.multiple_of(target * rhs_here, rhs_here), rhs_here), :],
            sol_box.at[slot], sol_send_sem.at[target], sol_sem.at[slot],
            device_id={"col": target})

    def send_sol(step, carry):
        sol_copy(lax.rem(col + step, cols), col).start()
        return carry

    lax.fori_loop(1, cols, send_sol, 0)
    sol_box[col] = full[pl.ds(pl.multiple_of(col * rhs_here, rhs_here), rhs_here), :]

    def receive_sol(step, carry):
        origin = lax.rem(col + cols - step, cols)
        sol_copy(origin, origin).wait_recv()
        return carry

    lax.fori_loop(1, cols, receive_sol, 0)
    taken = jnp.zeros((rhs_here, rows * slots), F32)
    for source in range(cols):
        piece = sol_box[source]
        root_out[:, source * width:(source + 1) * width] = piece
        taken = taken + dot_nn(piece.astype(BF16), hot[source * width:(source + 1) * width, :])
    for leaf_index in range(rows):
        take[leaf_index] = taken[:, leaf_index * slots:(leaf_index + 1) * slots]

    def take_copy(target, slot):
        return pltpu.make_async_remote_copy(
            take.at[target], take_box.at[slot], take_send_sem.at[target],
            take_sem.at[slot], device_id={"row": target})

    for step in range(1, rows):
        take_copy(lax.rem(row + step, rows), row).start()
    take_box[row] = take[row]
    for step in range(1, rows):
        source = lax.rem(row + step, rows)
        take_copy(source, source).wait_recv()
    picked = take_box[0]
    for source in range(1, rows):
        picked = picked + take_box[source]
    picked = jnp.where(live, picked, 0.0).astype(BF16)
    leaf_out[...] = solved[...] - dot_nn(picked, interpolation[...])

    for step in range(1, rows):
        target = lax.rem(row + step, rows)
        skel_copy(target, target).wait_send()
        take_copy(target, row).wait_send()

        @pl.when(row + step < rows)
        def _():
            vec_copy(0, row + step, row).wait_send()

        @pl.when(row - step >= 0)
        def _():
            vec_copy(1, row - step, row).wait_send()

    def drain(step, carry):
        target = lax.rem(col + step, cols)
        assem_copy(target, col).wait_send()
        sol_copy(target, col).wait_send()
        rs_copy(2, target, col).wait_send()

        @pl.when(row > 0)
        def _():
            rs_copy(0, target, col).wait_send()

        @pl.when(row < rows - 1)
        def _():
            rs_copy(1, target, col).wait_send()

        return carry

    lax.fori_loop(1, cols, drain, 0)


def on_device(
    rows, cols,
    leaf_rhs, leaf_inverse, interpolation, ranks, skeleton_rows, root_rows, root_rhs, root_factor
):
    _, rhs_here, leaf = leaf_rhs.shape
    slots = skeleton_rows.shape[1]
    section = root_rhs.shape[1]
    width = section // cols
    rhs = rhs_here * cols
    factor = jnp.transpose(root_factor, (1, 0, 2))
    vmem = pl.BlockSpec(memory_space=pltpu.VMEM)
    smem = pl.BlockSpec(memory_space=pltpu.SMEM)
    hbm = pl.BlockSpec(memory_space=pl.ANY)
    dma = pltpu.SemaphoreType.DMA
    leaf_solution, root_solution = pl.pallas_call(
        functools.partial(kernel, rows, cols),
        out_shape=(
            jax.ShapeDtypeStruct((rhs_here, leaf), F32),
            jax.ShapeDtypeStruct((rhs_here, section), F32),
        ),
        in_specs=[smem, vmem, hbm, vmem, vmem, vmem, vmem, hbm],
        out_specs=(vmem, vmem),
        scratch_shapes=[
            pltpu.VMEM((leaf, leaf), BF16),
            pltpu.VMEM((rows, section, width), BF16),
            pltpu.VMEM((section, rows * slots), BF16),
            pltpu.VMEM((rhs_here, leaf), F32),
            pltpu.VMEM((rows, rhs_here, slots), F32),
            pltpu.VMEM((cols, rhs_here, width), F32),
            pltpu.VMEM((cols, rhs_here, width), F32),
            pltpu.VMEM((3, rhs, width), BF16),
            pltpu.VMEM((2, rows, rhs, width), BF16),
            pltpu.VMEM((cols, rhs, width), F32),
            pltpu.VMEM((3, cols, rhs, width), BF16),
            pltpu.VMEM((3, cols, rhs, width), BF16),
            pltpu.VMEM((rhs, width), F32),
            pltpu.VMEM((rhs, width), F32),
            pltpu.VMEM((cols, rhs_here, width), F32),
            pltpu.VMEM((rows, rhs_here, slots), F32),
            pltpu.VMEM((rows, rhs_here, slots), F32),
            dma, dma,
            dma((rows,)), dma((rows,)), dma((cols,)), dma((cols,)),
            dma((2, rows)), dma((2, rows)), dma((3, cols)), dma((3, cols)),
            dma((cols,)), dma((cols,)), dma((rows,)), dma((rows,)),
        ],
        compiler_params=pltpu.CompilerParams(
            collective_id=0, has_side_effects=True, vmem_limit_bytes=56 * 1024 * 1024),
        name="root_solve",
    )(
        ranks, leaf_rhs[0], leaf_inverse[0], interpolation[0], skeleton_rows, root_rows,
        root_rhs, factor,
    )
    return leaf_solution[None], root_solution


def solution(mesh):
    in_specs = (
        P("row", "col", None),
        P("row", None, None),
        P("row", None, None),
        P("row"),
        P("row", None),
        P(),
        P("col", "row"),
        P("row", None, "col"),
    )
    out_specs = (P("row", "col", None), P("col", "row"))
    return jax.shard_map(
        functools.partial(on_device, mesh.shape["row"], mesh.shape["col"]),
        mesh=mesh, in_specs=in_specs, out_specs=out_specs, check_vma=False,
    )
```

time: 1070 us -> 143 us (0.13)
  blocking collectives: 708 us -> 0 us
  waiting for transfers between devices: 229 us -> 0 us
  Pallas kernels: 0 us -> 122 us
  matrix products: 44.4 us -> 0 us
  local copies, waits for them, and re-layouts: 51.4 us -> 19.3 us
  between operations: 15 us -> 1.29 us
  starting transfers between devices: 11.4 us -> 0 us
    all_gather x13 -> x0, blocking collectives: 695 us -> none  [the longest x7 537 us: on_device(): lax.all_gather(arrived, 'col', axis=1, tiled=True)]
    psum x7 -> x0, waiting for transfers between devices: 221 us -> none  [from_root(): return lax.psum(kept, axis)]
    pallas_call x0 -> x1, Pallas kernels: none -> 122 us  [on_device(): pl.pallas_call(functools.partial(kernel, rows, cols), out_shape=(jax.Shap...]
    dot_general x13 -> x0, matrix products: 44.4 us -> none  [the longest x11 37.8 us: product_rows(): lax.dot_general(left_rows, factor_rows, (((1,), (1,)), ((), ())), preferr...]
    all_to_all x4 -> x0, local copies, waits for them, and re-layouts: 39.3 us -> none  [the longest x2 38.1 us: on_device(): lax.all_to_all(root_factor, 'col', split_axis=0, concat_axis=2, tiled=True)]
    unnamed x10 -> x3, local copies, waits for them, and re-layouts: 1.85 us -> 19.3 us
    all_to_all x1 -> x0, blocking collectives: 13.5 us -> none  [on_device(): lax.all_to_all(assembled, 'col', split_axis=1, concat_axis=0, tiled=True)]
    all_to_all x2 -> x0, starting transfers between devices: 11.1 us -> none  [the longest x1 5.74 us: on_device(): lax.all_to_all(root_factor, 'col', split_axis=0, concat_axis=2, tiled=True)]
  transfers between devices with their start and end apart: 9 -> 0, of which waited for: 8 -> 0; matrix products, arithmetic and copies ran while one was open for 0% -> 0% of each run, Pallas kernels for 0% -> 0%
where the time goes in v1:
time: 143 us
  Pallas kernels  122 us (85%)
  local copies, waits for them, and re-layouts  19.3 us (13%)
    pallas_call x1, Pallas kernels, on_device(): pl.pallas_call(functools.partial(kernel, rows, cols), out_shape=(jax.Shap...  122 us
    unnamed x3, local copies, waits for them, and re-layouts  19.3 us

profile of v1, /device:TPU:0, one launch (start us, length us, event | category | flops | bytes accessed | tf_op | source)
XLA Modules:
  0.0 143.0 jit_solution(11295912810278382492)
XLA Ops:
  1.3 16.2 %copy.12 = bf16[4096,4,512]{2,0,1:T(8,128)(2,1)} copy(bf16[4096,4,512]{2,1,0:T(4,128)(2,1)} %param.15) | data formatting | bytes 33554432 | tf_op args[7]
  17.5 122.4 %root_solve.1 = (f32[8,2048]{1,0:T(8,128)}, f32[8,4096]{1,0:T(8,128)}) custom-call(s32[1]{0:T(128)S(6)} %copy.15.ranks, bf16[8,2048]{1,0:T(8,128)(2,1)} %bitcast.11, bf16[2048,2048]{1,0:T(8,128)(2,1)} %bitcast.8, bf16[128,2048]{1,0:T(8,128)(2,1)} %bitcast.9, s32[1,128]{1,0:T(1,128)} %skeleton_rows.1, s32[4,128]{1,0:T(4,128)} %root_rows.1, ...), custom_call_target="tpu_custom_call" | custom-call | tf_op jit(solution)/shard_map/root_solve/pallas_call | solution.py:314
  139.9 1.5 %copy.16 = f32[1,8,2048]{2,1,0:T(8,128)} copy(f32[1,8,2048]{2,1,0:T(8,128)} %bitcast.10) | data formatting | bytes 131072
  141.4 1.6 %copy.17 = f32[8,4096]{1,0:T(8,128)} copy(f32[8,4096]{1,0:T(8,128)} %get-tuple-element.9) | data formatting | bytes 262144

commit v2 on v1

--- a/solution.py
+++ b/solution.py
@@ -23,6 +23,9 @@
     high = value.astype(BF16)
     low = (value - high.astype(F32)).astype(BF16)
     return jnp.concatenate([high, low], axis=0)
+
+
+GROUPS = 2
 
 
 def kernel(
@@ -44,7 +47,6 @@
     load_inverse = pltpu.make_async_copy(leaf_inverse, inverse_v, inverse_sem)
     load_inverse.start()
     load_factor = pltpu.make_async_copy(factor, factor_v, factor_sem)
-    load_factor.start()
 
     barrier = pltpu.get_barrier_semaphore()
     for step in range(1, rows):
@@ -67,6 +69,7 @@
     live = lax.broadcasted_iota(jnp.int32, (rhs_here, slots), 1) < ranks[0]
 
     load_inverse.wait()
+    load_factor.start()
     leaf_step = 256
     here = leaf_rhs[...]
     skeleton = jnp.zeros((2 * rhs_here, slots), F32)
@@ -129,10 +132,16 @@
 
     load_factor.wait()
 
-    def vec_copy(kind, target, slot):
-        return pltpu.make_async_remote_copy(
-            vec_send.at[kind], vec_box.at[kind, slot], vec_send_sem.at[kind, target],
-            vec_sem.at[kind, slot], device_id={"row": target})
+    share = rhs_here * cols // GROUPS
+
+    def part_of(group):
+        return pl.ds(group * share, share)
+
+    def vec_copy(kind, group, target, slot):
+        return pltpu.make_async_remote_copy(
+            vec_send.at[kind, part_of(group)], vec_box.at[kind, slot, part_of(group)],
+            vec_send_sem.at[kind, target, group], vec_sem.at[kind, slot, group],
+            device_id={"row": target})
 
     def clear():
         def body(part, carry):
@@ -143,83 +152,104 @@
     def block(source, part):
         return factor_v[source, pl.ds(pl.multiple_of(part * width, width), width), :]
 
-    def gather_in(kind, source):
-        vec_copy(kind, source, source).wait_recv()
+    def gather_in(kind, group, source):
+        vec_copy(kind, group, source, source).wait_recv()
 
         def body(part, carry):
-            acc[part] += dot_nt(vec_box[kind, source], block(source, part))
+            acc[part, part_of(group), :] += dot_nt(
+                vec_box[kind, source, part_of(group), :], block(source, part))
             return carry
 
-        lax.fori_loop(0, cols, body, 0)
-
-    def rs_copy(phase, target, slot):
-        return pltpu.make_async_remote_copy(
-            stage.at[phase, target], box.at[phase, slot], rs_send_sem.at[phase, target],
-            rs_sem.at[phase, slot], device_id={"col": target})
-
-    def reduce_scatter(phase, vector, source, with_acc):
+        lax.fori_loop(0, cols, body, 0, unroll=True)
+
+    def rs_copy(phase, group, target, slot):
+        return pltpu.make_async_remote_copy(
+            stage.at[phase, target, part_of(group)], box.at[phase, slot, part_of(group)],
+            rs_send_sem.at[phase, target, group], rs_sem.at[phase, slot, group],
+            device_id={"col": target})
+
+    def scatter(phase, group, vector, source, with_acc):
         def send(step, carry):
             target = lax.rem(col + step, cols)
-            part = dot_nt(vector(), block(source, target))
+            part = dot_nt(vector, block(source, target))
             if with_acc:
-                part = part + acc[target]
-            stage[phase, target] = part.astype(BF16)
-            rs_copy(phase, target, col).start()
+                part = part + acc[target, part_of(group), :]
+            stage[phase, target, part_of(group), :] = part.astype(BF16)
+            rs_copy(phase, group, target, col).start()
             return carry
 
-        lax.fori_loop(1, cols, send, 0)
-        total = dot_nt(vector(), block(source, col))
+        lax.fori_loop(1, cols, send, 0, unroll=True)
+        total = dot_nt(vector, block(source, col))
         if with_acc:
-            total = total + acc[col]
-        full[...] = total
-
-        def receive(step, carry):
+            total = total + acc[col, part_of(group), :]
+        full[part_of(group), :] = total
+
+    def collect(phase, group):
+        total = full[part_of(group), :]
+        for step in range(1, cols):
             origin = lax.rem(col + cols - step, cols)
-            rs_copy(phase, origin, origin).wait_recv()
-            full[...] += box[phase, origin].astype(F32)
-            return carry
-
-        lax.fori_loop(1, cols, receive, 0)
+            rs_copy(phase, group, origin, origin).wait_recv()
+            total = total + box[phase, origin, part_of(group), :].astype(F32)
+        return total
+
+    def send_forward(group):
+        vec_send[0, part_of(group), :] = kept[part_of(group), :].astype(BF16)
+        for step in range(1, rows):
+            @pl.when(row + step < rows)
+            def _():
+                vec_copy(0, group, row + step, row).start()
+
+    @pl.when(row == 0)
+    def _():
+        for group in range(GROUPS):
+            send_forward(group)
 
     @pl.when(row > 0)
     def _():
         clear()
 
         def body(source, carry):
-            gather_in(0, source)
+            for group in range(GROUPS):
+                gather_in(0, group, source)
             return carry
 
         lax.fori_loop(0, row - 1, body, 0)
-        vec_copy(0, row - 1, row - 1).wait_recv()
-        reduce_scatter(0, lambda: vec_box[0, row - 1], row - 1, True)
-        kept[...] = kept[...] - full[...]
-
-    vec_send[0] = kept[...].astype(BF16)
-    for step in range(1, rows):
-        @pl.when(row + step < rows)
+        for group in range(GROUPS):
+            vec_copy(0, group, row - 1, row - 1).wait_recv()
+            scatter(0, group, vec_box[0, row - 1, part_of(group), :], row - 1, True)
+
+        @pl.when(row < rows - 1)
         def _():
-            vec_copy(0, row + step, row).start()
+            for group in range(GROUPS):
+                kept[part_of(group), :] -= collect(0, group)
+                send_forward(group)
 
     @pl.when(row < rows - 1)
     def _():
         clear()
 
         def body(step, carry):
-            gather_in(1, rows - 1 - step)
+            for group in range(GROUPS):
+                gather_in(1, group, rows - 1 - step)
             return carry
 
         lax.fori_loop(0, rows - 2 - row, body, 0)
-        vec_copy(1, row + 1, row + 1).wait_recv()
-        reduce_scatter(1, lambda: vec_box[1, row + 1], row + 1, True)
-        kept[...] = kept[...] - full[...]
-
-    vec_send[2] = kept[...].astype(BF16)
-    reduce_scatter(2, lambda: vec_send[2], row, False)
-    vec_send[1] = full[...].astype(BF16)
-    for step in range(1, rows):
-        @pl.when(row - step >= 0)
-        def _():
-            vec_copy(1, row - step, row).start()
+        for group in range(GROUPS):
+            vec_copy(1, group, row + 1, row + 1).wait_recv()
+            scatter(1, group, vec_box[1, row + 1, part_of(group), :], row + 1, True)
+
+    last = jnp.where(row == rows - 1, 0, 1)
+    for group in range(GROUPS):
+        low = (kept[part_of(group), :] - collect(last, group)).astype(BF16)
+        scatter(2, group, low, row, False)
+    for group in range(GROUPS):
+        total = collect(2, group)
+        full[part_of(group), :] = total
+        vec_send[1, part_of(group), :] = total.astype(BF16)
+        for step in range(1, rows):
+            @pl.when(row - step >= 0)
+            def _():
+                vec_copy(1, group, row - step, row).start()
 
     def sol_copy(target, slot):
         return pltpu.make_async_remote_copy(
@@ -270,27 +300,29 @@
         skel_copy(target, target).wait_send()
         take_copy(target, row).wait_send()
 
-        @pl.when(row + step < rows)
-        def _():
-            vec_copy(0, row + step, row).wait_send()
-
-        @pl.when(row - step >= 0)
-        def _():
-            vec_copy(1, row - step, row).wait_send()
+        for group in range(GROUPS):
+            @pl.when(row + step < rows)
+            def _():
+                vec_copy(0, group, row + step, row).wait_send()
+
+            @pl.when(row - step >= 0)
+            def _():
+                vec_copy(1, group, row - step, row).wait_send()
 
     def drain(step, carry):
         target = lax.rem(col + step, cols)
         assem_copy(target, col).wait_send()
         sol_copy(target, col).wait_send()
-        rs_copy(2, target, col).wait_send()
-
-        @pl.when(row > 0)
-        def _():
-            rs_copy(0, target, col).wait_send()
-
-        @pl.when(row < rows - 1)
-        def _():
-            rs_copy(1, target, col).wait_send()
+        for group in range(GROUPS):
+            rs_copy(2, group, target, col).wait_send()
+
+            @pl.when(row > 0)
+            def _():
+                rs_copy(0, group, target, col).wait_send()
+
+            @pl.when(row < rows - 1)
+            def _():
+                rs_copy(1, group, target, col).wait_send()
 
         return carry
 
@@ -327,7 +359,7 @@
             pltpu.VMEM((rows, rhs_here, slots), F32),
             pltpu.VMEM((cols, rhs_here, width), F32),
             pltpu.VMEM((cols, rhs_here, width), F32),
-            pltpu.VMEM((3, rhs, width), BF16),
+            pltpu.VMEM((2, rhs, width), BF16),
             pltpu.VMEM((2, rows, rhs, width), BF16),
             pltpu.VMEM((cols, rhs, width), F32),
             pltpu.VMEM((3, cols, rhs, width), BF16),
@@ -339,7 +371,8 @@
             pltpu.VMEM((rows, rhs_here, slots), F32),
             dma, dma,
             dma((rows,)), dma((rows,)), dma((cols,)), dma((cols,)),
-            dma((2, rows)), dma((2, rows)), dma((3, cols)), dma((3, cols)),
+            dma((2, rows, GROUPS)), dma((2, rows, GROUPS)),
+            dma((3, cols, GROUPS)), dma((3, cols, GROUPS)),
             dma((cols,)), dma((cols,)), dma((rows,)), dma((rows,)),
         ],
         compiler_params=pltpu.CompilerParams(

time: 143 us -> 127 us (0.89)
  Pallas kernels: 122 us -> 106 us
    pallas_call x1, Pallas kernels: 122 us -> 106 us  [on_device(): pl.pallas_call(functools.partial(kernel, rows, cols), out_shape=(jax.Shap...]
where the time goes in v2:
time: 127 us; the launch traced here: 126 us
  Pallas kernels  106 us (83%)
  local copies, waits for them, and re-layouts  19.3 us (15%)
  between operations  1.29 us (1%)
    pallas_call x1, Pallas kernels, on_device(): pl.pallas_call(functools.partial(kernel, rows, cols), out_shape=(jax.Shap...  106 us
    unnamed x3, local copies, waits for them, and re-layouts  19.3 us

profile of v2, /device:TPU:0, one launch (start us, length us, event | category | flops | bytes accessed | tf_op | source)
XLA Modules:
  0.0 126.2 jit_solution(16188380481619835690)
XLA Ops:
  1.3 16.2 %copy.12 = bf16[4096,4,512]{2,0,1:T(8,128)(2,1)} copy(bf16[4096,4,512]{2,1,0:T(4,128)(2,1)} %param.15) | data formatting | bytes 33554432 | tf_op args[7]
  17.5 105.6 %root_solve.1 = (f32[8,2048]{1,0:T(8,128)}, f32[8,4096]{1,0:T(8,128)}) custom-call(s32[1]{0:T(128)S(6)} %copy.15.ranks, bf16[8,2048]{1,0:T(8,128)(2,1)} %bitcast.11, bf16[2048,2048]{1,0:T(8,128)(2,1)} %bitcast.8, bf16[128,2048]{1,0:T(8,128)(2,1)} %bitcast.9, s32[1,128]{1,0:T(1,128)} %skeleton_rows.1, s32[4,128]{1,0:T(4,128)} %root_rows.1, ...), custom_call_target="tpu_custom_call" | custom-call | tf_op jit(solution)/shard_map/root_solve/pallas_call | solution.py:346
  123.1 1.5 %copy.16 = f32[1,8,2048]{2,1,0:T(8,128)} copy(f32[1,8,2048]{2,1,0:T(8,128)} %bitcast.10) | data formatting | bytes 131072
  124.6 1.6 %copy.17 = f32[8,4096]{1,0:T(8,128)} copy(f32[8,4096]{1,0:T(8,128)} %get-tuple-element.9) | data formatting | bytes 262144

commit v3 on v2

--- a/solution.py
+++ b/solution.py
@@ -33,7 +33,7 @@
     ranks, leaf_rhs, leaf_inverse, interpolation, skeleton_rows, root_rows, root_rhs, factor,
     leaf_out, root_out,
     inverse_v, factor_v, hot, solved, skel_box, assem, assem_box, vec_send, vec_box,
-    acc, stage, box, kept, full, sol_box, take, take_box,
+    acc, stage, box, kept, own, full, sol_box, take, take_box,
     inverse_sem, factor_sem, skel_send_sem, skel_sem, assem_send_sem, assem_sem,
     vec_send_sem, vec_sem, rs_send_sem, rs_sem, sol_send_sem, sol_sem, take_send_sem, take_sem,
 ):
@@ -127,19 +127,32 @@
         return carry
 
     lax.fori_loop(1, cols, take_assem, 0)
-    for source in range(cols):
-        kept[source * rhs_here:(source + 1) * rhs_here, :] = assem_box[source]
+    share = rhs_here * cols // GROUPS
+    lanes = kept.shape[2]
+    fold = lanes // share
+    tall = width // fold
+
+    def packed(value):
+        return jnp.concatenate(
+            [value[at * tall:(at + 1) * tall, :] for at in range(fold)], axis=1)
+
+    def unpacked(value):
+        return jnp.concatenate(
+            [value[:, at * share:(at + 1) * share] for at in range(fold)], axis=0)
+
+    tile = jnp.concatenate([assem_box[source] for source in range(cols)], axis=0)
+    if tile.shape[0] < lanes:
+        tile = jnp.concatenate(
+            [tile, jnp.zeros((lanes - tile.shape[0], width), F32)], axis=0)
+    turned = jnp.transpose(tile)
+    for group in range(GROUPS):
+        kept[group] = packed(turned[:, group * share:(group + 1) * share])
 
     load_factor.wait()
 
-    share = rhs_here * cols // GROUPS
-
-    def part_of(group):
-        return pl.ds(group * share, share)
-
     def vec_copy(kind, group, target, slot):
         return pltpu.make_async_remote_copy(
-            vec_send.at[kind, part_of(group)], vec_box.at[kind, slot, part_of(group)],
+            vec_send.at[kind, group], vec_box.at[kind, slot, group],
             vec_send_sem.at[kind, target, group], vec_sem.at[kind, slot, group],
             device_id={"row": target})
 
@@ -152,48 +165,52 @@
     def block(source, part):
         return factor_v[source, pl.ds(pl.multiple_of(part * width, width), width), :]
 
+    def vector_of(kind, group, source):
+        return unpacked(vec_box[kind, source, group].astype(F32)).astype(BF16)
+
     def gather_in(kind, group, source):
         vec_copy(kind, group, source, source).wait_recv()
 
+        vector = vector_of(kind, group, source)
+
         def body(part, carry):
-            acc[part, part_of(group), :] += dot_nt(
-                vec_box[kind, source, part_of(group), :], block(source, part))
+            acc[part, group] += packed(dot_nn(block(source, part), vector))
             return carry
 
         lax.fori_loop(0, cols, body, 0, unroll=True)
 
     def rs_copy(phase, group, target, slot):
         return pltpu.make_async_remote_copy(
-            stage.at[phase, target, part_of(group)], box.at[phase, slot, part_of(group)],
+            stage.at[phase, target, group], box.at[phase, slot, group],
             rs_send_sem.at[phase, target, group], rs_sem.at[phase, slot, group],
             device_id={"col": target})
 
     def scatter(phase, group, vector, source, with_acc):
         def send(step, carry):
             target = lax.rem(col + step, cols)
-            part = dot_nt(vector, block(source, target))
+            part = packed(dot_nn(block(source, target), vector))
             if with_acc:
-                part = part + acc[target, part_of(group), :]
-            stage[phase, target, part_of(group), :] = part.astype(BF16)
+                part = part + acc[target, group]
+            stage[phase, target, group] = part.astype(BF16)
             rs_copy(phase, group, target, col).start()
             return carry
 
         lax.fori_loop(1, cols, send, 0, unroll=True)
-        total = dot_nt(vector, block(source, col))
+        total = packed(dot_nn(block(source, col), vector))
         if with_acc:
-            total = total + acc[col, part_of(group), :]
-        full[part_of(group), :] = total
+            total = total + acc[col, group]
+        own[group] = total
 
     def collect(phase, group):
-        total = full[part_of(group), :]
+        total = own[group]
         for step in range(1, cols):
             origin = lax.rem(col + cols - step, cols)
             rs_copy(phase, group, origin, origin).wait_recv()
-            total = total + box[phase, origin, part_of(group), :].astype(F32)
+            total = total + box[phase, origin, group].astype(F32)
         return total
 
     def send_forward(group):
-        vec_send[0, part_of(group), :] = kept[part_of(group), :].astype(BF16)
+        vec_send[0, group] = kept[group].astype(BF16)
         for step in range(1, rows):
             @pl.when(row + step < rows)
             def _():
@@ -216,12 +233,12 @@
         lax.fori_loop(0, row - 1, body, 0)
         for group in range(GROUPS):
             vec_copy(0, group, row - 1, row - 1).wait_recv()
-            scatter(0, group, vec_box[0, row - 1, part_of(group), :], row - 1, True)
+            scatter(0, group, vector_of(0, group, row - 1), row - 1, True)
 
         @pl.when(row < rows - 1)
         def _():
             for group in range(GROUPS):
-                kept[part_of(group), :] -= collect(0, group)
+                kept[group] -= collect(0, group)
                 send_forward(group)
 
     @pl.when(row < rows - 1)
@@ -236,20 +253,26 @@
         lax.fori_loop(0, rows - 2 - row, body, 0)
         for group in range(GROUPS):
             vec_copy(1, group, row + 1, row + 1).wait_recv()
-            scatter(1, group, vec_box[1, row + 1, part_of(group), :], row + 1, True)
+            scatter(1, group, vector_of(1, group, row + 1), row + 1, True)
 
     last = jnp.where(row == rows - 1, 0, 1)
     for group in range(GROUPS):
-        low = (kept[part_of(group), :] - collect(last, group)).astype(BF16)
+        low = unpacked(kept[group] - collect(last, group)).astype(BF16)
         scatter(2, group, low, row, False)
     for group in range(GROUPS):
         total = collect(2, group)
-        full[part_of(group), :] = total
-        vec_send[1, part_of(group), :] = total.astype(BF16)
+        own[group] = total
+        vec_send[1, group] = total.astype(BF16)
         for step in range(1, rows):
             @pl.when(row - step >= 0)
             def _():
                 vec_copy(1, group, row - step, row).start()
+
+    turned = jnp.concatenate([unpacked(own[group]) for group in range(GROUPS)], axis=1)
+    if turned.shape[1] < lanes:
+        turned = jnp.concatenate(
+            [turned, jnp.zeros((width, lanes - turned.shape[1]), F32)], axis=1)
+    full[...] = jnp.transpose(turned)[:full.shape[0], :]
 
     def sol_copy(target, slot):
         return pltpu.make_async_remote_copy(
@@ -338,6 +361,8 @@
     section = root_rhs.shape[1]
     width = section // cols
     rhs = rhs_here * cols
+    lanes = 128
+    folded = (GROUPS, rhs * width // (GROUPS * lanes), lanes)
     factor = jnp.transpose(root_factor, (1, 0, 2))
     vmem = pl.BlockSpec(memory_space=pltpu.VMEM)
     smem = pl.BlockSpec(memory_space=pltpu.SMEM)
@@ -359,12 +384,13 @@
             pltpu.VMEM((rows, rhs_here, slots), F32),
             pltpu.VMEM((cols, rhs_here, width), F32),
             pltpu.VMEM((cols, rhs_here, width), F32),
-            pltpu.VMEM((2, rhs, width), BF16),
-            pltpu.VMEM((2, rows, rhs, width), BF16),
-            pltpu.VMEM((cols, rhs, width), F32),
-            pltpu.VMEM((3, cols, rhs, width), BF16),
-            pltpu.VMEM((3, cols, rhs, width), BF16),
-            pltpu.VMEM((rhs, width), F32),
+            pltpu.VMEM((2,) + folded, BF16),
+            pltpu.VMEM((2, rows) + folded, BF16),
+            pltpu.VMEM((cols,) + folded, F32),
+            pltpu.VMEM((3, cols) + folded, BF16),
+            pltpu.VMEM((3, cols) + folded, BF16),
+            pltpu.VMEM(folded, F32),
+            pltpu.VMEM(folded, F32),
             pltpu.VMEM((rhs, width), F32),
             pltpu.VMEM((cols, rhs_here, width), F32),
             pltpu.VMEM((rows, rhs_here, slots), F32),

time: 127 us -> 140 us (1.10)
  Pallas kernels: 106 us -> 120 us
    pallas_call x1, Pallas kernels: 106 us -> 120 us  [on_device(): pl.pallas_call(functools.partial(kernel, rows, cols), out_shape=(jax.Shap...]
where the time goes in v3:
time: 140 us
  Pallas kernels  120 us (86%)
  local copies, waits for them, and re-layouts  19.3 us (14%)
    pallas_call x1, Pallas kernels, on_device(): pl.pallas_call(functools.partial(kernel, rows, cols), out_shape=(jax.Shap...  120 us
    unnamed x3, local copies, waits for them, and re-layouts  19.3 us

profile of v3, /device:TPU:0, one launch (start us, length us, event | category | flops | bytes accessed | tf_op | source)
XLA Modules:
  0.0 140.1 jit_solution(16069507111543521498)
XLA Ops:
  1.3 16.2 %copy.12 = bf16[4096,4,512]{2,0,1:T(8,128)(2,1)} copy(bf16[4096,4,512]{2,1,0:T(4,128)(2,1)} %param.15) | data formatting | bytes 33554432 | tf_op args[7]
  17.5 119.6 %root_solve.1 = (f32[8,2048]{1,0:T(8,128)}, f32[8,4096]{1,0:T(8,128)}) custom-call(s32[1]{0:T(128)S(6)} %copy.15.ranks, bf16[8,2048]{1,0:T(8,128)(2,1)} %bitcast.11, bf16[2048,2048]{1,0:T(8,128)(2,1)} %bitcast.8, bf16[128,2048]{1,0:T(8,128)(2,1)} %bitcast.9, s32[1,128]{1,0:T(1,128)} %skeleton_rows.1, s32[4,128]{1,0:T(4,128)} %root_rows.1, ...), custom_call_target="tpu_custom_call" | custom-call | tf_op jit(solution)/shard_map/root_solve/pallas_call | solution.py:371
  137.1 1.5 %copy.16 = f32[1,8,2048]{2,1,0:T(8,128)} copy(f32[1,8,2048]{2,1,0:T(8,128)} %bitcast.10) | data formatting | bytes 131072
  138.5 1.6 %copy.17 = f32[8,4096]{1,0:T(8,128)} copy(f32[8,4096]{1,0:T(8,128)} %get-tuple-element.9) | data formatting | bytes 262144

commit v4 on v2

--- a/solution.py
+++ b/solution.py
@@ -25,7 +25,7 @@
     return jnp.concatenate([high, low], axis=0)
 
 
-GROUPS = 2
+GROUPS = 1
 
 
 def kernel(
@@ -169,7 +169,8 @@
             device_id={"col": target})
 
     def scatter(phase, group, vector, source, with_acc):
-        def send(step, carry):
+        def send(turn, carry):
+            step = cols // 2 + (2 * (turn % 2) - 1) * (turn // 2)
             target = lax.rem(col + step, cols)
             part = dot_nt(vector, block(source, target))
             if with_acc:

time: 127 us -> 140 us (1.10)
  Pallas kernels: 106 us -> 120 us
    pallas_call x1, Pallas kernels: 106 us -> 120 us  [on_device(): pl.pallas_call(functools.partial(kernel, rows, cols), out_shape=(jax.Shap...]
where the time goes in v4:
time: 140 us
  Pallas kernels  120 us (86%)
  local copies, waits for them, and re-layouts  19.3 us (14%)
    pallas_call x1, Pallas kernels, on_device(): pl.pallas_call(functools.partial(kernel, rows, cols), out_shape=(jax.Shap...  120 us
    unnamed x3, local copies, waits for them, and re-layouts  19.3 us

profile of v4, /device:TPU:0, one launch (start us, length us, event | category | flops | bytes accessed | tf_op | source)
XLA Modules:
  0.0 140.1 jit_solution(11582728412938084023)
XLA Ops:
  1.3 16.2 %copy.12 = bf16[4096,4,512]{2,0,1:T(8,128)(2,1)} copy(bf16[4096,4,512]{2,1,0:T(4,128)(2,1)} %param.15) | data formatting | bytes 33554432 | tf_op args[7]
  17.5 119.6 %root_solve.1 = (f32[8,2048]{1,0:T(8,128)}, f32[8,4096]{1,0:T(8,128)}) custom-call(s32[1]{0:T(128)S(6)} %copy.15.ranks, bf16[8,2048]{1,0:T(8,128)(2,1)} %bitcast.11, bf16[2048,2048]{1,0:T(8,128)(2,1)} %bitcast.8, bf16[128,2048]{1,0:T(8,128)(2,1)} %bitcast.9, s32[1,128]{1,0:T(1,128)} %skeleton_rows.1, s32[4,128]{1,0:T(4,128)} %root_rows.1, ...), custom_call_target="tpu_custom_call" | custom-call | tf_op jit(solution)/shard_map/root_solve/pallas_call | solution.py:347
  137.1 1.5 %copy.16 = f32[1,8,2048]{2,1,0:T(8,128)} copy(f32[1,8,2048]{2,1,0:T(8,128)} %bitcast.10) | data formatting | bytes 131072
  138.6 1.6 %copy.17 = f32[8,4096]{1,0:T(8,128)} copy(f32[8,4096]{1,0:T(8,128)} %get-tuple-element.9) | data formatting | bytes 262144
